TPU v7x, 128 devices: a whole 4x4x4 slice. The times are simulated.
128 devices in a mesh: graph: 32 (over z, y, core), mp: 4 (over x).
Axes of the slice: x: 4, y: 4, z: 4, core: 2. Of those that a mesh axis runs over, the one named last changes fastest.
Arguments:
- node_features: bfloat16 [65536, 512], P('graph'), may hold values from -6 to 6
- w_qkv: bfloat16 [3, 512, 512], P(None, None, 'mp'), may hold values from -0.25 to 0.25
- w_out: bfloat16 [512, 512], P('mp'), may hold values from -0.25 to 0.25
- head_scale: float32 [8], P('mp'), may hold values from 1 to 100
- norm_gain: float32 [512], replicated, may hold values from 0.1 to 1.9
- router: bfloat16 [512, 64], replicated, may hold values from -0.5 to 0.5
- w_gate: bfloat16 [64, 512, 2048], P('graph', None, 'mp'), may hold values from -0.25 to 0.25
- w_up: bfloat16 [64, 512, 2048], P('graph', None, 'mp'), may hold values from -0.25 to 0.25
- w_down: bfloat16 [64, 2048, 512], P('graph', 'mp'), may hold values from -0.25 to 0.25
- neighbor_blocks: int32 [512, 12], P('graph'), may hold values from 0 to 511, as said below
- expert_ids: int32 [65536, 1], P('graph'), may hold values from 0 to 63; in each aligned block of 2048 rows (0 to 2047, 2048 to 4095, ...) at most 96 rows name the same one
Outputs:
- attn_out: bfloat16 [65536, 512], P('graph', 'mp')
- layer_out: bfloat16 [65536, 512], P('graph', 'mp')
Inputs may be any that keep to these rules, and one draw needn't show every extreme that they name: `neighbor_blocks`: row b lists distinct blocks: b itself, 3 other blocks of the same index of graph (blocks of part p are p * 16 to p * 16 + 15), then 8 blocks of other parts. Among all rows of one part, at most 2 distinct blocks come from any one other part, and every part reaches 2 from some other part. `expert_ids`: among the rows of one index of graph, at most 96 name one expert, a bound that some block reaches.
All inputs are finite; a program needn't handle non-finite values.
Results may differ from a plain program's by a relative error of at most 0.012.
The roundings to bfloat16 on the way count: a program that leaves them out, or rounds other values in their place, can miss the bound.
Values may be sent and summed in bfloat16 or wider, within the bound.
No kernel may reach another device: no remote copies, remote signals or barrier semaphores. Data moves between devices by JAX's collectives and lax.ppermute only.
A program may use at most 128 MiB of HBM per device.

v0:
```python
import math
import jax
import jax.numpy as jnp
from jax import lax
from jax.sharding import PartitionSpec as P

HEAD_DIM = 64
ROWS_BLK = 128
CAP_H = 2


def unit_rms(values):
    return values * lax.rsqrt(jnp.mean(values * values, axis=-1, keepdims=True) + 1e-06)


def make_work(gate_weights, up_weights, down_weights, tokens):
    gate_part = jnp.einsum(
        "gesd,edf->gesf", tokens, gate_weights, preferred_element_type=jnp.float32
    )
    up_part = jnp.einsum("gesd,edf->gesf", tokens, up_weights, preferred_element_type=jnp.float32)
    hidden = (jax.nn.silu(gate_part) * up_part).astype(jnp.bfloat16)
    return jnp.einsum("gesf,efd->gesd", hidden, down_weights, preferred_element_type=jnp.float32)


def on_device(
    node_features,
    w_qkv,
    w_out,
    head_scale,
    norm_gain,
    router,
    w_gate,
    w_up,
    w_down,
    neighbor_blocks,
    expert_ids,
):
    graph_count = lax.axis_size("graph")
    own_part = lax.axis_index("graph")
    column_start = lax.axis_index("mp") * w_qkv.shape[2]
    rows = node_features.shape[0]
    width = node_features.shape[1]
    local_width = w_qkv.shape[2]
    local_heads = local_width // HEAD_DIM
    blocks = rows // ROWS_BLK
    query = jnp.dot(node_features, w_qkv[0], preferred_element_type=jnp.float32).reshape(
        rows, local_heads, HEAD_DIM
    )
    keys = jnp.dot(node_features, w_qkv[1], preferred_element_type=jnp.float32).reshape(
        rows, local_heads, HEAD_DIM
    )
    values = jnp.dot(node_features, w_qkv[2], preferred_element_type=jnp.float32)
    scaled = (unit_rms(query) * (head_scale / math.sqrt(HEAD_DIM))[None, :, None]).astype(
        jnp.bfloat16
    )
    key_unit = unit_rms(keys).astype(jnp.bfloat16).reshape(blocks, ROWS_BLK, local_width)
    value_rows = values.astype(jnp.bfloat16).reshape(blocks, ROWS_BLK, local_width)
    key_value = jnp.concatenate([key_unit, value_rows], axis=2)
    entries = neighbor_blocks.reshape(-1)
    owner = entries // blocks
    local_index = entries % blocks
    listed = jnp.arange(entries.shape[0], dtype=jnp.int32)
    repeated = jnp.any(
        (entries[:, None] == entries[None, :]) & (listed[None, :] < listed[:, None]), axis=1
    )
    wanted = (owner != own_part) & jnp.logical_not(repeated)
    part_ids = jnp.arange(graph_count, dtype=jnp.int32)
    owner_hit = ((owner[:, None] == part_ids[None, :]) & wanted[:, None]).astype(jnp.int32)
    position = jnp.sum((jnp.cumsum(owner_hit, axis=0) - owner_hit) * owner_hit, axis=1)
    slot_hit = (position[:, None] == jnp.arange(CAP_H, dtype=jnp.int32)[None, :]).astype(jnp.int32)
    requests = (
        jnp.sum(
            owner_hit[:, :, None] * slot_hit[:, None, :] * (local_index + 1)[:, None, None], axis=0
        )
        - 1
    )
    incoming = lax.all_to_all(requests, "graph", split_axis=0, concat_axis=0, tiled=True)
    outgoing = key_value[jnp.maximum(incoming, 0)]
    halo_rows = lax.all_to_all(outgoing, "graph", split_axis=0, concat_axis=0, tiled=True)
    halo_ids = jnp.where(requests >= 0, part_ids[:, None] * blocks + requests, -1).reshape(-1)
    pool_ids = jnp.concatenate([own_part * blocks + jnp.arange(blocks, dtype=jnp.int32), halo_ids])
    key_pool = jnp.concatenate(
        [key_value, halo_rows.reshape(-1, ROWS_BLK, 2 * local_width)], axis=0
    )
    pool_slots = jnp.arange(pool_ids.shape[0], dtype=jnp.int32)
    slot_index = jnp.sum(
        jnp.where(
            neighbor_blocks[:, :, None] == pool_ids[None, None, :], pool_slots[None, None, :], 0
        ),
        axis=2,
    )
    gathered = key_pool[slot_index].reshape(blocks, -1, 2 * local_width)
    key_part = gathered[:, :, :local_width].reshape(blocks, -1, local_heads, HEAD_DIM)
    value_part = gathered[:, :, local_width:].reshape(blocks, -1, local_heads, HEAD_DIM)
    query_blocks = scaled.reshape(blocks, ROWS_BLK, local_heads, HEAD_DIM)
    scores = jnp.einsum(
        "bqhd,bkhd->bhqk", query_blocks, key_part, preferred_element_type=jnp.float32
    )
    largest = jnp.max(scores, axis=-1, keepdims=True)
    expo = jnp.exp(scores - largest)
    weights = (expo / jnp.sum(expo, axis=-1, keepdims=True)).astype(jnp.bfloat16)
    attended = jnp.einsum(
        "bhqk,bkhd->bqhd", weights, value_part, preferred_element_type=jnp.float32
    )
    attended = attended.astype(jnp.bfloat16).reshape(rows, local_width)
    partial_value = jnp.dot(attended, w_out, preferred_element_type=jnp.float32)
    total = lax.psum(partial_value, "mp")
    mixed = node_features.astype(jnp.float32) + total
    normed = (unit_rms(mixed) * norm_gain).astype(jnp.bfloat16)
    attn_cols = lax.dynamic_slice_in_dim(total, column_start, local_width, 1)
    mixed_cols = lax.dynamic_slice_in_dim(mixed, column_start, local_width, 1)
    experts = router.shape[1]
    capacity = 3 * rows // experts
    routed = expert_ids[:, 0]
    chosen = routed[:, None] == jnp.arange(experts, dtype=jnp.int32)[None, :]
    logits = jnp.dot(normed, router, preferred_element_type=jnp.float32)
    gate = jax.nn.sigmoid(jnp.sum(jnp.where(chosen, logits, 0.0), axis=1))
    row_ids = jnp.arange(rows, dtype=jnp.int32)
    earlier = (row_ids[:, None] > row_ids[None, :]).astype(jnp.bfloat16)
    before = jnp.dot(earlier, chosen.astype(jnp.bfloat16), preferred_element_type=jnp.float32)
    rank_in = jnp.sum(jnp.where(chosen, before, 0.0), axis=1).astype(jnp.int32)
    target = routed * capacity + rank_in
    buffer = jnp.zeros((experts * capacity, width), jnp.bfloat16).at[target].set(normed)
    buffer = buffer.reshape(graph_count, w_gate.shape[0], capacity, width)
    produced = make_work(
        w_gate,
        w_up,
        w_down,
        lax.all_to_all(buffer, "graph", split_axis=0, concat_axis=0, tiled=True),
    )
    back = lax.all_to_all(
        produced.astype(jnp.bfloat16), "graph", split_axis=0, concat_axis=0, tiled=True
    ).astype(produced.dtype)
    mine = back.reshape(-1, width)[target]
    expert_cols = lax.psum_scatter(
        mine.astype(jnp.bfloat16), "mp", scatter_dimension=1, tiled=True
    ).astype(jnp.float32)
    layer_out = (mixed_cols + gate[:, None] * expert_cols).astype(jnp.bfloat16)
    return (attn_cols.astype(jnp.bfloat16), layer_out)


def solution(mesh):
    placed = (
        P("graph", None),
        P(None, None, "mp"),
        P("mp", None),
        P("mp"),
        P(),
        P(),
        P("graph", None, "mp"),
        P("graph", None, "mp"),
        P("graph", "mp", None),
        P("graph", None),
        P("graph", None),
    )
    return jax.shard_map(
        on_device,
        mesh=mesh,
        in_specs=placed,
        out_specs=(P("graph", "mp"), P("graph", "mp")),
        check_vma=False,
    )
```

profile of v0, /device:TPU:1, one launch (start us, length us, event | category | flops | bytes accessed | tf_op | source)
XLA Modules:
  0.0 512.2 jit_solution(45271411930314655)
XLA Ops:
  7.2 0.0 copy-start
  7.2 0.9 reshape.272
  8.1 0.2 fusion.52
  8.3 0.6 reduce-window.6
  8.9 0.2 slice_reduce_fusion
  9.2 0.1 bitcast_bitcast_fusion
  9.3 0.1 multiply_reduce_fusion.3
  9.4 0.7 copy.52
  10.1 9.6 %all-to-all-start = ((s32[32,1,2]{2,1,0:T(1,128)}), s32[32,1,2]{2,1,0:T(1,128)S(1)}, u32[]{:S(2)}, u32[]{:S(2)}) async-start(s32[32,1,2]{2,1,0:T(1,128)} %copy.52), calls=%async_computation | async-start | bytes 32768 | tf_op jit(solution)/shard_map/all_to_all | solution.py:77
  19.7 1.0 slice_bitcast_fusion
  20.7 0.1 copy.48
  20.8 2.3 convolution_convert_fusion
  23.2 2.6 multiply_reduce_fusion.2
  25.8 0.1 multiply_convert_fusion.2
  25.9 0.1 copy.72
  26.0 0.5 copy.49
  26.5 0.1 pad_maximum_fusion.1
  26.6 0.0 all-to-all-done
  26.7 0.1 maximum_reduce_fusion
  26.7 0.1 reshape.289
  26.8 0.4 copy-done.3
  27.3 2.8 gather_fusion
  30.1 7.6 %all-to-all-start.1 = ((bf16[32,2,128,256]{3,2,1,0:T(8,128)(2,1)}), bf16[32,2,128,256]{3,2,1,0:T(8,128)(2,1)}, u32[]{:S(2)}, u32[]{:S(2)}) async-start(bf16[32,2,128,256]{3,2,1,0:T(8,128)(2,1)} %bitcast.145), calls=%async_computation.1 | async-start | bytes 8388608 | tf_op jit(solution)/shard_map/all_to_all | solution.py:79
  37.6 0.2 all-reduce.3.cloned.1.call-start
  37.9 0.1 copy.53
  38.0 0.1 copy.54
  38.0 0.1 select_n.65
  38.2 0.1 pad_add_fusion
  38.2 0.4 select_reduce_fusion
  38.6 0.1 copy.55
  38.7 0.1 reshape.297
  38.8 0.1 copy.57
  39.0 1.9 multiply_reduce_fusion.1
  40.9 47.0 %all-to-all-done.1 = bf16[32,2,128,256]{3,2,1,0:T(8,128)(2,1)} async-done(((bf16[32,2,128,256]{3,2,1,0:T(8,128)(2,1)}), bf16[32,2,128,256]{3,2,1,0:T(8,128)(2,1)}, u32[]{:S(2)}, u32[]{:S(2)}) %all-to-all-start.1) | async-done | bytes 4194336 | tf_op jit(solution)/shard_map/all_to_all | solution.py:79
  87.9 5.5 %pad_maximum_fusion = bf16[80,128,256]{2,1,0:T(8,128)(2,1)} fusion(bf16[64,128,256]{2,1,0:T(8,128)(2,1)} %bitcast.9, bf16[16,128,128]{2,1,0:T(8,128)(2,1)} %bitcast.151, bf16[16,128,128]{2,1,0:T(8,128)(2,1)} %copy-done.3), kind=kLoop, calls=%fused_computation.24 | loop fusion | flops 15728640 | bytes 10485760 | tf_op jit(solution)/shard_map/concatenate | solution.py:82
  93.4 10.7 %gather_fusion.1 = bf16[192,128,256]{2,1,0:T(8,128)(2,1)} fusion(bf16[80,128,256]{2,1,0:T(8,128)(2,1)} %pad_maximum_fusion, s32[1024]{0:T(1024)S(1)} %pad_clamp_fusion), kind=kCustom, calls=%fused_computation.1 | custom fusion | bytes 25166592 | tf_op jit(solution)/shard_map/gather | solution.py:92
  104.2 11.7 %fusion.71 = (bf16[16,1536,128]{2,1,0:T(8,128)(2,1)}, bf16[16,1536,128]{2,1,0:T(8,128)(2,1)}) fusion(bf16[16,1536,256]{2,1,0:T(8,128)(2,1)} %bitcast.143), kind=kLoop, calls=%fused_computation.114 | loop fusion | bytes 25165824 | tf_op jit(solution)/shard_map/slice | solution.py:93
  115.9 8.7 %copy.58 = bf16[16,1536,128]{1,2,0:T(8,128)(2,1)} copy(bf16[16,1536,128]{2,1,0:T(8,128)(2,1)} %get-tuple-element.6) | data formatting | bytes 12582912 | tf_op jit(solution)/shard_map/slice | solution.py:93
  124.5 8.6 %copy.56 = bf16[16,1536,128]{1,2,0:T(8,128)(2,1)} copy(bf16[16,1536,128]{2,1,0:T(8,128)(2,1)} %get-tuple-element.7) | data formatting | bytes 12582912 | tf_op jit(solution)/shard_map/slice | solution.py:94
  133.2 7.8 %fusion.72 = f32[16,2,128]{2,1,0:T(2,128)S(1)} fusion(bf16[16,1536,2,64]{1,3,2,0:T(8,128)(2,1)} %bitcast.147, f32[2048,2,64]{0,2,1:T(8,128)} %get-tuple-element.15, f32[2]{0:T(128)S(1)} %broadcast_multiply_fusion, f32[2048,2]{0,1:T(2,128)S(1)} %add_rsqrt_fusion), kind=kOutput, calls=%fused_computation.115 | convolution fusion | flops 818677248 | bytes 7372808 | tf_op jit(solution)/shard_map/sub | solution.py:100
  141.0 12.9 %fusion.29 = bf16[16,128,2,64]{1,3,2,0:T(8,128)(2,1)} fusion(bf16[16,1536,2,64]{1,3,2,0:T(8,128)(2,1)} %bitcast.149, f32[16,2,128]{2,1,0:T(2,128)S(1)} %fusion.72, bf16[16,1536,2,64]{1,3,2,0:T(8,128)(2,1)} %bitcast.148, f32[2048,2,64]{0,2,1:T(8,128)} %get-tuple-element.15, f32[2]{0:T(128)S(1)} %broadcast_multiply_fusion, f32[2048,2]{0,1:T(2,128)S(1)} %add_rsqrt_fusion), kind=kOutput, calls=%fused_computation.39 | convolution fusion | flops 1630541312 | bytes 14188552 | tf_op jit(solution)/shard_map/bhqk,bkhd->bqhd/dot_general | solution.py:102
  153.9 1.4 copy.60
  155.3 2.7 fusion.37
  157.9 0.0 all-reduce.3.cloned.1.call-update
  158.0 1.7 fusion.31
  159.7 90.8 %all-reduce.3.cloned.1.call-done = f32[2048,512]{1,0:T(8,128)} async-done(((f32[2048,512]{1,0:T(8,128)}), f32[2048,512]{1,0:T(8,128)}) %all-reduce.3.cloned.1.call-update) | async-done | bytes 4194320 | tf_op jit(solution)/shard_map/psum | solution.py:107
  250.5 4.7 multiply_reduce_fusion
  255.2 14.8 %scatter_custom_fusion = bf16[6144,512]{1,0:T(8,128)(2,1)} fusion(s32[2048]{0:T(1024)S(1)} %bitcast.160, bf16[]{:T(256)} %constant.85.clone.1, f32[2048,512]{1,0:T(8,128)} %get-tuple-element.3, f32[512]{0:T(512)S(1)} %copy-done.9, f32[2048]{0:T(1024)S(1)} %add_rsqrt_fusion.2), kind=kCustom, calls=%fused_computation.28 | custom fusion | flops 3145728 | bytes 10496002 | tf_op jit(solution)/shard_map/scatter | solution.py:123
  270.0 81.1 %all_to_all.21 = bf16[32,2,96,512]{3,2,1,0:T(8,128)(2,1)S(1)} all-to-all(bf16[32,2,96,512]{3,2,1,0:T(8,128)(2,1)} %bitcast.144), channel_id=1, replica_groups=mesh['graph'=32,'mp'=4] {'graph'}, dimensions={0} | all-to-all | bytes 12582912 | tf_op jit(solution)/shard_map/all_to_all | solution.py:129
  351.0 2.6 copy-done.2
  353.6 6.5 %fusion.9 = f32[2,32,96,512]{3,2,1,0:T(8,128)} fusion(bf16[32,2,96,512]{3,2,1,0:T(8,128)(2,1)S(1)} %all_to_all.21, bf16[2,512,512]{2,1,0:T(8,128)(2,1)S(1)} %copy-done), kind=kOutput, calls=%fused_computation.20 | convolution fusion | flops 3221225472 | bytes 19922944 | tf_op jit(solution)/shard_map/gesd,edf->gesf/dot_general | solution.py:20
  360.1 14.0 %convert_bitcast_fusion = bf16[32,2,96,512]{3,2,0,1:T(8,128)(2,1)} fusion(f32[2,32,96,512]{3,2,1,0:T(8,128)} %fusion.9, bf16[32,2,96,512]{3,2,1,0:T(8,128)(2,1)} %copy-done.2, bf16[2,512,512]{2,1,0:T(8,128)(2,1)S(1)} %copy-done.10, bf16[2,512,512]{2,1,0:T(8,128)(2,1)S(1)} %copy-done.11), kind=kOutput, calls=%fused_computation.18 | convolution fusion | flops 6464471040 | bytes 27262976 | tf_op jit(solution)/shard_map/gesf,efd->gesd/dot_general | solution.py:22
  374.1 6.2 %copy.63 = bf16[32,2,96,512]{3,2,1,0:T(8,128)(2,1)} copy(bf16[32,2,96,512]{3,2,0,1:T(8,128)(2,1)} %convert_bitcast_fusion) | data formatting | bytes 12582912 | tf_op jit(solution)/shard_map/convert_element_type | solution.py:132
  380.2 4.9 all-to-all-start.3
  385.1 0.0 reduce-scatter.4.cloned.1.call-start
  385.2 73.0 %all-to-all-done.3 = bf16[32,2,96,512]{3,2,1,0:T(8,128)(2,1)} async-done(((bf16[32,2,96,512]{3,2,1,0:T(8,128)(2,1)}), bf16[32,2,96,512]{3,2,1,0:T(8,128)(2,1)}, u32[]{:S(2)}, u32[]{:S(2)}) %all-to-all-start.3) | async-done | bytes 6291488 | tf_op jit(solution)/shard_map/all_to_all | solution.py:131
  458.2 11.2 %gather_fusion.2 = bf16[2048,512]{1,0:T(8,128)(2,1)S(1)} fusion(bf16[6144,512]{1,0:T(8,128)(2,1)} %bitcast.118, s32[2048]{0:T(1024)S(1)} %broadcast_clamp_fusion), kind=kCustom, calls=%fused_computation.2 | custom fusion | bytes 4202496 | tf_op jit(solution)/shard_map/gather | solution.py:134
  469.4 2.5 copy.67
  471.9 0.0 reduce-scatter.4.cloned.1.call-update
  471.9 3.1 fusion.30
  475.0 2.1 dynamic-slice_convert_fusion
  477.1 24.6 %reduce-scatter.4.cloned.1.call-done = bf16[128,2048]{1,0:T(8,128)(2,1)} async-done(((bf16[512,2048]{1,0:T(8,128)(2,1)}), bf16[128,2048]{1,0:T(8,128)(2,1)}) %reduce-scatter.4.cloned.1.call-update) | async-done | bytes 524304
  501.6 1.3 copy.68
  502.9 2.4 add_convert_fusion
  (46 shorter events, 0.3 us)
Async XLA Ops:
  7.2 346.5 %copy-start = (bf16[2,512,512]{2,1,0:T(8,128)(2,1)S(1)}, bf16[2,512,512]{2,1,0:T(8,128)(2,1)}, u32[]{:S(2)}) copy-start(bf16[2,512,512]{2,1,0:T(8,128)(2,1)} %param.18) | copy-start | bytes 3145732
  10.1 16.6 %all-to-all-start = ((s32[32,1,2]{2,1,0:T(1,128)}), s32[32,1,2]{2,1,0:T(1,128)S(1)}, u32[]{:S(2)}, u32[]{:S(2)}) async-start(s32[32,1,2]{2,1,0:T(1,128)} %copy.52), calls=%async_computation | async-start | bytes 32768 | tf_op jit(solution)/shard_map/all_to_all | solution.py:77
  23.1 3.7 copy-start.4
  26.5 0.8 copy-start.3
  30.1 7.8 %copy-start.8 = (s32[16,12]{1,0:T(8,128)S(1)}, s32[16,12]{1,0:T(8,128)}, u32[]{:S(2)}) copy-start(s32[16,12]{1,0:T(8,128)} %param.20) | copy-start | bytes 2308
  30.1 8.9 %copy-start.12 = (f32[2]{0:T(128)S(1)}, f32[2]{0:T(128)}, u32[]{:S(2)}) copy-start(f32[2]{0:T(128)} %param.14) | copy-start | bytes 28
  30.1 8.9 %copy-start.1 = (bf16[2048,512]{1,0:T(8,128)(2,1)S(1)}, bf16[2048,512]{1,0:T(8,128)(2,1)}, u32[]{:S(2)}) copy-start(bf16[2048,512]{1,0:T(8,128)(2,1)} %param.11) | copy-start | bytes 6291460
  30.1 57.8 %all-to-all-start.1 = ((bf16[32,2,128,256]{3,2,1,0:T(8,128)(2,1)}), bf16[32,2,128,256]{3,2,1,0:T(8,128)(2,1)}, u32[]{:S(2)}, u32[]{:S(2)}) async-start(bf16[32,2,128,256]{3,2,1,0:T(8,128)(2,1)} %bitcast.145), calls=%async_computation.1 | async-start | bytes 8388608 | tf_op jit(solution)/shard_map/all_to_all | solution.py:79
  37.6 212.9 %all-reduce.3.cloned.1.call-start = ((), (), s32[]{:S(2)}) async-start(), calls=%async_computation.5 | async-start | bytes 8388608 | tf_op jit(solution)/shard_map/psum | solution.py:107
  141.0 14.3 %copy-start.5 = (bf16[128,512]{1,0:T(8,128)(2,1)S(1)}, bf16[128,512]{1,0:T(8,128)(2,1)}, u32[]{:S(2)}) copy-start(bf16[128,512]{1,0:T(8,128)(2,1)} %param.13) | copy-start | bytes 393220
  153.9 4.1 copy-start.7
  159.6 95.6 %copy-start.9 = (f32[512]{0:T(512)S(1)}, f32[512]{0:T(512)}, u32[]{:S(2)}) copy-start(f32[512]{0:T(512)} %param.15) | copy-start | bytes 6148
  351.0 2.6 copy-start.2
  353.6 6.5 %copy-start.10 = (bf16[2,512,512]{2,1,0:T(8,128)(2,1)S(1)}, bf16[2,512,512]{2,1,0:T(8,128)(2,1)}, u32[]{:S(2)}) copy-start(bf16[2,512,512]{2,1,0:T(8,128)(2,1)} %param.19) | copy-start | bytes 3145732
  353.6 6.5 %copy-start.11 = (bf16[2,512,512]{2,1,0:T(8,128)(2,1)S(1)}, bf16[2,512,512]{2,1,0:T(8,128)(2,1)}, u32[]{:S(2)}) copy-start(bf16[2,512,512]{2,1,0:T(8,128)(2,1)} %param.17) | copy-start | bytes 3145732
  380.2 77.9 %all-to-all-start.3 = ((bf16[32,2,96,512]{3,2,1,0:T(8,128)(2,1)}), bf16[32,2,96,512]{3,2,1,0:T(8,128)(2,1)}, u32[]{:S(2)}, u32[]{:S(2)}) async-start(bf16[32,2,96,512]{3,2,1,0:T(8,128)(2,1)} %copy.63), calls=%async_computation.3 | async-start | bytes 12582912 | tf_op jit(solution)/shard_map/all_to_all | solution.py:131
  385.1 116.5 %reduce-scatter.4.cloned.1.call-start = ((), (), s32[]{:S(2)}) async-start(), calls=%async_computation.6 | async-start | bytes 2621440
  469.4 2.5 copy-start.6
Sparse Core Ops, SparseCore 0:
  158.1 92.3 all-reduce.2
  472.0 29.5 reduce-scatter.3
where the time goes:
time: 513 us; the launch traced here: 512 us
  waiting for transfers between devices  235 us (46%)
  blocking collectives  81.1 us (16%)
  local copies, waits for them, and re-layouts  74.3 us (14%)
  matrix products  55.3 us (11%)
  other arithmetic  29.3 us (6%)
  starting transfers between devices  22.3 us (4%)
  between operations  14.5 us (3%)
    psum x1, waiting for transfers between devices, on_device(): total = lax.psum(partial_value, 'mp')  90.8 us
    all_to_all x1, blocking collectives, on_device(): lax.all_to_all(buffer, 'graph', split_axis=0, concat_axis=0, tiled=True)  81.1 us
    all_to_all x1, waiting for transfers between devices, on_device(): lax.all_to_all(produced.astype(jnp.bfloat16), 'graph', split_axis=0, conc...  73 us
    all_to_all x1, waiting for transfers between devices, on_device(): lax.all_to_all(outgoing, 'graph', split_axis=0, concat_axis=0, tiled=True)  47 us
    unnamed x3, waiting for transfers between devices  24.6 us
    slice x2, local copies, waits for them, and re-layouts, on_device(): gathered[:, :, :local_width].reshape(blocks, -1, local_heads, HEAD_DIM)  20.4 us
    scatter x1, other arithmetic, on_device(): jnp.zeros((experts * capacity, width), jnp.bfloat16).at[target].set(normed)  14.8 us
    dot_general x1, matrix products, make_work(): jnp.einsum('gesf,efd->gesd', hidden, down_weights, preferred_element_type...  14 us
  transfers between devices with their start and end apart: 5, of which 4 were waited for; matrix products, arithmetic and copies ran while one was open for 3% of the time, Pallas kernels for 0%

commit v1 on v0

--- a/solution.py
+++ b/solution.py
@@ -1,3 +1,4 @@
+import functools
 import math
 import jax
 import jax.numpy as jnp
@@ -7,6 +8,20 @@
 HEAD_DIM = 64
 ROWS_BLK = 128
 CAP_H = 2
+
+
+def check_tables(packet, net_axis):
+    nd = lax.psum(1, net_axis)
+    even = lambda outcome_arr: [(dev_i, dev_i ^ outcome_arr) for dev_i in range(nd)]
+    current_arr = packet
+    for k0 in range(nd.bit_length() - 1):
+        later = even(1 << k0)
+        v_now = lax.ppermute(current_arr, net_axis, later)
+        current_arr = current_arr + v_now
+    return current_arr
+
+
+_reach_heads = functools.partial(check_tables, net_axis="mp")
 
 
 def unit_rms(values):
@@ -104,7 +119,7 @@
     )
     attended = attended.astype(jnp.bfloat16).reshape(rows, local_width)
     partial_value = jnp.dot(attended, w_out, preferred_element_type=jnp.float32)
-    total = lax.psum(partial_value, "mp")
+    total = _reach_heads(partial_value)
     mixed = node_features.astype(jnp.float32) + total
     normed = (unit_rms(mixed) * norm_gain).astype(jnp.bfloat16)
     attn_cols = lax.dynamic_slice_in_dim(total, column_start, local_width, 1)

time: 513 us -> 615 us (1.20)
  waiting for transfers between devices: 235 us -> 317 us
  local copies, waits for them, and re-layouts: 74.3 us -> 99.7 us
  other arithmetic: 29.3 us -> 18.2 us
  blocking collectives: 81.1 us -> 87.9 us
    ppermute x0 -> x2, waiting for transfers between devices: none -> 170 us  [check_tables(): v_now = lax.ppermute(current_arr, net_axis, later)]
    psum x1 -> x0, waiting for transfers between devices: 90.8 us -> none  [on_device(): total = lax.psum(partial_value, 'mp')]
    reduce_scatter x0 -> x1, waiting for transfers between devices: none -> 26.8 us  [on_device(): lax.psum_scatter(mine.astype(jnp.bfloat16), 'mp', scatter_dimension=1, ti...]
    unnamed x3 -> x1, waiting for transfers between devices: 24.6 us -> 0.02 us
    scatter x1 -> x0, other arithmetic: 14.8 us -> none  [on_device(): jnp.zeros((experts * capacity, width), jnp.bfloat16).at[target].set(normed)]
    scatter x0 -> x1, local copies, waits for them, and re-layouts: none -> 13.8 us  [on_device(): jnp.zeros((experts * capacity, width), jnp.bfloat16).at[target].set(normed)]
    all_to_all x1, blocking collectives: 81.1 us -> 87.9 us  [on_device(): lax.all_to_all(buffer, 'graph', split_axis=0, concat_axis=0, tiled=True)]
    gather x1 -> x2, local copies, waits for them, and re-layouts: 11.2 us -> 16.8 us  [on_device(): mine = back.reshape(-1, width)[target]]
  transfers between devices with their start and end apart: 5 -> 6, of which waited for: 4 -> 5; matrix products, arithmetic and copies ran while one was open for 3% -> 3% of each run, Pallas kernels for 0% -> 0%
where the time goes in v1:
time: 615 us; the launch traced here: 614 us
  waiting for transfers between devices  317 us (52%)
  local copies, waits for them, and re-layouts  99.7 us (16%)
  blocking collectives  87.9 us (14%)
  matrix products  50.9 us (8%)
  starting transfers between devices  26.1 us (4%)
  other arithmetic  18.2 us (3%)
  between operations  14.4 us (2%)
    ppermute x2, waiting for transfers between devices, check_tables(): v_now = lax.ppermute(current_arr, net_axis, later)  170 us
    all_to_all x1, blocking collectives, on_device(): lax.all_to_all(buffer, 'graph', split_axis=0, concat_axis=0, tiled=True)  87.9 us
    all_to_all x1, waiting for transfers between devices, on_device(): lax.all_to_all(produced.astype(jnp.bfloat16), 'graph', split_axis=0, conc...  73 us
    all_to_all x1, waiting for transfers between devices, on_device(): lax.all_to_all(outgoing, 'graph', split_axis=0, concat_axis=0, tiled=True)  47.1 us
    reduce_scatter x1, waiting for transfers between devices, on_device(): lax.psum_scatter(mine.astype(jnp.bfloat16), 'mp', scatter_dimension=1, ti...  26.8 us
    slice x2, local copies, waits for them, and re-layouts, on_device(): gathered[:, :, :local_width].reshape(blocks, -1, local_heads, HEAD_DIM)  20.4 us
    gather x2, local copies, waits for them, and re-layouts, on_device(): mine = back.reshape(-1, width)[target]  16.8 us
    dot_general x1, matrix products, make_work(): jnp.einsum('gesf,efd->gesd', hidden, down_weights, preferred_element_type...  14.1 us
  transfers between devices with their start and end apart: 6, of which 5 were waited for; matrix products, arithmetic and copies ran while one was open for 3% of the time, Pallas kernels for 0%

profile of v1, /device:TPU:1, one launch (start us, length us, event | category | flops | bytes accessed | tf_op | source)
XLA Modules:
  0.0 613.8 jit_solution(4490984794122186038)
XLA Ops:
  7.2 0.9 reshape.272
  8.1 0.2 fusion.52
  8.3 0.6 reduce-window.6
  8.9 0.2 slice_reduce_fusion
  9.3 0.1 multiply_reduce_fusion.3
  9.4 0.7 copy.66
  10.1 9.6 %all-to-all-start = ((s32[32,1,2]{2,1,0:T(1,128)}), s32[32,1,2]{2,1,0:T(1,128)S(1)}, u32[]{:S(2)}, u32[]{:S(2)}) async-start(s32[32,1,2]{2,1,0:T(1,128)} %copy.66), calls=%async_computation | async-start | bytes 32768 | tf_op jit(solution)/shard_map/all_to_all | solution.py:92
  19.7 1.0 slice_bitcast_fusion
  20.7 0.1 copy.62
  20.8 2.3 convolution_convert_fusion
  23.2 2.6 multiply_reduce_fusion.2
  25.8 0.1 multiply_convert_fusion.2
  25.9 0.1 copy.89
  26.0 0.5 copy.63
  26.5 0.1 pad_maximum_fusion.1
  26.7 0.1 reshape.289
  26.8 0.4 copy-done.5
  27.3 2.8 gather_fusion
  30.1 7.6 %all-to-all-start.1 = ((bf16[32,2,128,256]{3,2,1,0:T(8,128)(2,1)}), bf16[32,2,128,256]{3,2,1,0:T(8,128)(2,1)}, u32[]{:S(2)}, u32[]{:S(2)}) async-start(bf16[32,2,128,256]{3,2,1,0:T(8,128)(2,1)} %bitcast.144), calls=%async_computation.1 | async-start | bytes 8388608 | tf_op jit(solution)/shard_map/all_to_all | solution.py:94
  37.7 0.1 copy.67
  37.7 0.1 copy.68
  37.8 0.1 select_n.65
  38.0 0.4 select_reduce_fusion
  38.4 0.1 copy.69
  38.5 0.1 reshape.297
  38.6 0.1 copy.71
  38.7 1.9 multiply_reduce_fusion.1
  40.6 47.1 %all-to-all-done.1 = bf16[32,2,128,256]{3,2,1,0:T(8,128)(2,1)} async-done(((bf16[32,2,128,256]{3,2,1,0:T(8,128)(2,1)}), bf16[32,2,128,256]{3,2,1,0:T(8,128)(2,1)}, u32[]{:S(2)}, u32[]{:S(2)}) %all-to-all-start.1) | async-done | bytes 4194336 | tf_op jit(solution)/shard_map/all_to_all | solution.py:94
  87.8 5.5 pad_maximum_fusion
  93.3 10.7 %gather_fusion.1 = bf16[192,128,256]{2,1,0:T(8,128)(2,1)} fusion(bf16[80,128,256]{2,1,0:T(8,128)(2,1)} %pad_maximum_fusion, s32[1024]{0:T(1024)S(1)} %pad_clamp_fusion), kind=kCustom, calls=%fused_computation.1 | custom fusion | bytes 25166592 | tf_op jit(solution)/shard_map/gather | solution.py:107
  104.1 11.7 %fusion.71 = (bf16[16,1536,128]{2,1,0:T(8,128)(2,1)}, bf16[16,1536,128]{2,1,0:T(8,128)(2,1)}) fusion(bf16[16,1536,256]{2,1,0:T(8,128)(2,1)} %bitcast.142), kind=kLoop, calls=%fused_computation.114 | loop fusion | bytes 25165824 | tf_op jit(solution)/shard_map/slice | solution.py:108
  115.8 8.7 %copy.72 = bf16[16,1536,128]{1,2,0:T(8,128)(2,1)} copy(bf16[16,1536,128]{2,1,0:T(8,128)(2,1)} %get-tuple-element.15) | data formatting | bytes 12582912 | tf_op jit(solution)/shard_map/slice | solution.py:108
  124.4 8.6 %copy.70 = bf16[16,1536,128]{1,2,0:T(8,128)(2,1)} copy(bf16[16,1536,128]{2,1,0:T(8,128)(2,1)} %get-tuple-element.16) | data formatting | bytes 12582912 | tf_op jit(solution)/shard_map/slice | solution.py:109
  133.1 7.8 %fusion.72 = f32[16,2,128]{2,1,0:T(2,128)S(1)} fusion(bf16[16,1536,2,64]{1,3,2,0:T(8,128)(2,1)} %bitcast.145, f32[2048,2,64]{0,2,1:T(8,128)} %get-tuple-element.24, f32[2]{0:T(128)S(1)} %broadcast_multiply_fusion, f32[2048,2]{0,1:T(2,128)S(1)} %add_rsqrt_fusion), kind=kOutput, calls=%fused_computation.115 | convolution fusion | flops 818677248 | bytes 7372808 | tf_op jit(solution)/shard_map/sub | solution.py:115
  140.9 12.9 %fusion.29 = bf16[16,128,2,64]{1,3,2,0:T(8,128)(2,1)} fusion(bf16[16,1536,2,64]{1,3,2,0:T(8,128)(2,1)} %bitcast.147, f32[16,2,128]{2,1,0:T(2,128)S(1)} %fusion.72, bf16[16,1536,2,64]{1,3,2,0:T(8,128)(2,1)} %bitcast.146, f32[2048,2,64]{0,2,1:T(8,128)} %get-tuple-element.24, f32[2]{0:T(128)S(1)} %broadcast_multiply_fusion, f32[2048,2]{0,1:T(2,128)S(1)} %add_rsqrt_fusion), kind=kOutput, calls=%fused_computation.39 | convolution fusion | flops 1630541312 | bytes 14188552 | tf_op jit(solution)/shard_map/bhqk,bkhd->bqhd/dot_general | solution.py:117
  153.8 1.4 copy.74
  155.2 0.7 fusion.37
  155.9 1.3 collective-permute-start
  157.2 87.2 %collective-permute-done = f32[2048,512]{0,1:T(8,128)S(1)} collective-permute-done((f32[2048,512]{0,1:T(8,128)S(1)}, f32[2048,512]{0,1:T(8,128)S(1)}, u32[]{:S(2)}, u32[]{:S(2)}) %collective-permute-start) | collective-permute-done | bytes 4194336 | tf_op jit(solution)/shard_map/ppermute | solution.py:19
  244.4 2.7 add.143
  247.1 2.7 collective-permute-start.1
  249.9 2.5 copy.75
  252.4 1.7 fusion.31
  254.1 82.4 %collective-permute-done.1 = f32[2048,512]{0,1:T(8,128)} collective-permute-done((f32[2048,512]{0,1:T(8,128)}, f32[2048,512]{0,1:T(8,128)}, u32[]{:S(2)}, u32[]{:S(2)}) %collective-permute-start.1) | collective-permute-done | bytes 4194336 | tf_op jit(solution)/shard_map/ppermute | solution.py:19
  336.5 6.1 multiply_reduce_fusion
  342.6 2.0 copy-done.3
  344.6 0.4 multiply_convert_fusion
  345.0 2.5 copy.76
  347.5 13.8 %scatter_custom_fusion = bf16[6144,512]{1,0:T(8,128)(2,1)} fusion(s32[2048]{0:T(1024)S(1)} %bitcast.157, bf16[2048,512]{1,0:T(8,128)(2,1)} %copy.76, bf16[]{:T(256)} %constant.85.clone.1), kind=kCustom, calls=%fused_computation.28 | custom fusion | bytes 6291968 | tf_op jit(solution)/shard_map/scatter | solution.py:138
  361.3 87.9 %all_to_all.21 = bf16[32,2,96,512]{3,2,1,0:T(8,128)(2,1)S(1)} all-to-all(bf16[32,2,96,512]{3,2,1,0:T(8,128)(2,1)} %bitcast.143), channel_id=1, replica_groups=mesh['graph'=32,'mp'=4] {'graph'}, dimensions={0} | all-to-all | bytes 12582912 | tf_op jit(solution)/shard_map/all_to_all | solution.py:144
  449.2 2.6 copy-done.2
  451.7 6.4 %fusion.9 = f32[2,32,96,512]{3,2,1,0:T(8,128)} fusion(bf16[32,2,96,512]{3,2,1,0:T(8,128)(2,1)S(1)} %all_to_all.21, bf16[2,512,512]{2,1,0:T(8,128)(2,1)S(1)} %copy-done), kind=kOutput, calls=%fused_computation.20 | convolution fusion | flops 3221225472 | bytes 19922944 | tf_op jit(solution)/shard_map/gesd,edf->gesf/dot_general | solution.py:35
  458.2 14.1 %convert_bitcast_fusion = bf16[32,2,96,512]{3,2,0,1:T(8,128)(2,1)} fusion(f32[2,32,96,512]{3,2,1,0:T(8,128)} %fusion.9, bf16[32,2,96,512]{3,2,1,0:T(8,128)(2,1)} %copy-done.2, bf16[2,512,512]{2,1,0:T(8,128)(2,1)} %param.19, bf16[2,512,512]{2,1,0:T(8,128)(2,1)} %param.17), kind=kOutput, calls=%fused_computation.18 | convolution fusion | flops 6464471040 | bytes 27262976 | tf_op jit(solution)/shard_map/gesf,efd->gesd/dot_general | solution.py:37
  472.3 6.2 %copy.79 = bf16[32,2,96,512]{3,2,1,0:T(8,128)(2,1)} copy(bf16[32,2,96,512]{3,2,0,1:T(8,128)(2,1)} %convert_bitcast_fusion) | data formatting | bytes 12582912 | tf_op jit(solution)/shard_map/convert_element_type | solution.py:147
  478.5 4.9 all-to-all-start.3
  483.4 73.0 %all-to-all-done.3 = bf16[32,2,96,512]{3,2,1,0:T(8,128)(2,1)} async-done(((bf16[32,2,96,512]{3,2,1,0:T(8,128)(2,1)}), bf16[32,2,96,512]{3,2,1,0:T(8,128)(2,1)}, u32[]{:S(2)}, u32[]{:S(2)}) %all-to-all-start.3) | async-done | bytes 6291488 | tf_op jit(solution)/shard_map/all_to_all | solution.py:146
  556.4 12.8 %gather_fusion.2 = bf16[2048,512]{1,0:T(8,128)(2,1)} fusion(bf16[6144,512]{1,0:T(8,128)(2,1)} %bitcast.116, s32[2048]{0:T(1024)S(1)} %broadcast_clamp_fusion), kind=kCustom, calls=%fused_computation.2 | custom fusion | bytes 4202496 | tf_op jit(solution)/shard_map/gather | solution.py:149
  569.2 4.0 copy.80
  573.3 1.9 dynamic-slice_convert_fusion
  575.1 2.0 copy.81
  577.2 0.5 fusion.30
  577.7 26.8 %reduce-scatter.2.cloned.1.call-done = bf16[2048,128]{0,1:T(8,128)(2,1)} async-done(((bf16[2048,512]{0,1:T(8,128)(2,1)}), bf16[2048,128]{0,1:T(8,128)(2,1)}) %reduce-scatter.2.cloned.1.call-update) | async-done | bytes 524304 | tf_op jit(solution)/shard_map/reduce_scatter | solution.py:150
  604.5 1.5 add_convert_fusion
  606.0 1.0 copy.82
  (52 shorter events, 0.6 us)
Async XLA Ops:
  7.2 444.6 %copy-start = (bf16[2,512,512]{2,1,0:T(8,128)(2,1)S(1)}, bf16[2,512,512]{2,1,0:T(8,128)(2,1)}, u32[]{:S(2)}) copy-start(bf16[2,512,512]{2,1,0:T(8,128)(2,1)} %param.18) | copy-start | bytes 3145732
  10.1 16.6 %all-to-all-start = ((s32[32,1,2]{2,1,0:T(1,128)}), s32[32,1,2]{2,1,0:T(1,128)S(1)}, u32[]{:S(2)}, u32[]{:S(2)}) async-start(s32[32,1,2]{2,1,0:T(1,128)} %copy.66), calls=%async_computation | async-start | bytes 32768 | tf_op jit(solution)/shard_map/all_to_all | solution.py:92
  23.1 3.7 copy-start.6
  26.5 0.8 copy-start.5
  30.0 7.6 %copy-start.10 = (s32[16,12]{1,0:T(8,128)S(1)}, s32[16,12]{1,0:T(8,128)}, u32[]{:S(2)}) copy-start(s32[16,12]{1,0:T(8,128)} %param.20) | copy-start | bytes 2308
  30.0 8.7 %copy-start.12 = (f32[2]{0:T(128)S(1)}, f32[2]{0:T(128)}, u32[]{:S(2)}) copy-start(f32[2]{0:T(128)} %param.14) | copy-start | bytes 28
  30.1 8.7 %copy-start.1 = (bf16[2048,512]{1,0:T(8,128)(2,1)S(1)}, bf16[2048,512]{1,0:T(8,128)(2,1)}, u32[]{:S(2)}) copy-start(bf16[2048,512]{1,0:T(8,128)(2,1)} %param.11) | copy-start | bytes 6291460
  30.1 57.7 %all-to-all-start.1 = ((bf16[32,2,128,256]{3,2,1,0:T(8,128)(2,1)}), bf16[32,2,128,256]{3,2,1,0:T(8,128)(2,1)}, u32[]{:S(2)}, u32[]{:S(2)}) async-start(bf16[32,2,128,256]{3,2,1,0:T(8,128)(2,1)} %bitcast.144), calls=%async_computation.1 | async-start | bytes 8388608 | tf_op jit(solution)/shard_map/all_to_all | solution.py:94
  140.9 14.3 %copy-start.7 = (bf16[128,512]{1,0:T(8,128)(2,1)S(1)}, bf16[128,512]{1,0:T(8,128)(2,1)}, u32[]{:S(2)}) copy-start(bf16[128,512]{1,0:T(8,128)(2,1)} %param.13) | copy-start | bytes 393220
  155.9 96.5 %copy-start.9 = (s32[2048,1]{0,1:T(1,128)S(1)}, s32[2048,1]{0,1:T(1,128)}, u32[]{:S(2)}) copy-start(s32[2048,1]{0,1:T(1,128)} %param.21) | copy-start | bytes 24580
  155.9 88.5 %collective-permute-start = (f32[2048,512]{0,1:T(8,128)S(1)}, f32[2048,512]{0,1:T(8,128)S(1)}, u32[]{:S(2)}, u32[]{:S(2)}) collective-permute-start(f32[2048,512]{0,1:T(8,128)S(1)} %fusion.37), channel_id=1, source_target_pairs={{0,1},{1,0},{2,3},{3,2},{4,5},{5,4},{6,7},{7,6},{8,9},{9,8},{10,11... | collective-permute-start | bytes 12582920 | tf_op jit(solution)/shard_map/ppermute | solution.py:19
  247.1 89.3 %collective-permute-start.1 = (f32[2048,512]{0,1:T(8,128)}, f32[2048,512]{0,1:T(8,128)}, u32[]{:S(2)}, u32[]{:S(2)}) collective-permute-start(f32[2048,512]{0,1:T(8,128)} %add.143), channel_id=1, source_target_pairs={{0,2},{1,3},{2,0},{3,1},{4,6},{5,7},{6,4},{7,5},{8,10},{9,11},{10,... | collective-permute-start | bytes 12582920 | tf_op jit(solution)/shard_map/ppermute | solution.py:19
  252.4 84.1 %copy-start.4 = (bf16[2048,512]{0,1:T(8,128)(2,1)S(1)}, bf16[2048,512]{0,1:T(8,128)(2,1)}, u32[]{:S(2)}) copy-start(bf16[2048,512]{0,1:T(8,128)(2,1)} %copy.75) | copy-start | bytes 6291460
  254.1 90.5 %copy-start.11 = (f32[512]{0:T(512)S(1)}, f32[512]{0:T(512)}, u32[]{:S(2)}) copy-start(f32[512]{0:T(512)} %param.15) | copy-start | bytes 6148
  342.6 2.0 copy-start.3
  449.2 2.6 copy-start.2
  478.5 77.9 %all-to-all-start.3 = ((bf16[32,2,96,512]{3,2,1,0:T(8,128)(2,1)}), bf16[32,2,96,512]{3,2,1,0:T(8,128)(2,1)}, u32[]{:S(2)}, u32[]{:S(2)}) async-start(bf16[32,2,96,512]{3,2,1,0:T(8,128)(2,1)} %copy.79), calls=%async_computation.3 | async-start | bytes 12582912 | tf_op jit(solution)/shard_map/all_to_all | solution.py:146
  483.4 121.1 %reduce-scatter.2.cloned.1.call-start = ((), (), s32[]{:S(2)}) async-start(), calls=%async_computation.5 | async-start | bytes 2621440 | tf_op jit(solution)/shard_map/reduce_scatter | solution.py:150
  569.2 8.0 %copy-start.8 = (bf16[512,64]{0,1:T(8,128)(2,1)S(1)}, bf16[512,64]{0,1:T(8,128)(2,1)}, u32[]{:S(2)}) copy-start(bf16[512,64]{0,1:T(8,128)(2,1)} %param.16) | copy-start | bytes 196612
Sparse Core Ops, SparseCore 0:
  573.4 31.0 reduce-scatter.1
